TPU v7x, 32 devices: a whole 2x2x4 slice. The times are simulated.
32 devices in a mesh: ctx: 8 (over z, x), tp: 4 (over y, core).
Axes of the slice: x: 2, y: 2, z: 4, core: 2. Of those that a mesh axis runs over, the one named last changes fastest.
Arguments:
- normed_input: bfloat16 [4096, 4096], P('ctx'), may hold values from -12 to 12
- w_query: bfloat16 [4096, 2048], P(None, 'tp'), may hold values from -0.09375 to 0.09375
- key_weight: bfloat16 [4096, 512], P(None, 'tp'), may hold values from -0.09375 to 0.09375
- value_weight: bfloat16 [4096, 512], P(None, 'tp'), may hold values from -0.09375 to 0.09375
- output_weight: bfloat16 [4096, 2048], P(None, 'tp'), may hold values from -0.125 to 0.125
- output_cotangent: bfloat16 [4096, 4096], P('ctx'), may hold values from -6 to 6
- piece_doc: int32 [512], replicated, may hold values from 0 to 31, as said below
- piece_offset: int32 [512], replicated, may hold values from 0 to 480, as said below
- doc_owner: int32 [32], replicated, may hold values from 0 to 7, as said below
Outputs:
- grad_in: bfloat16 [4096, 4096], P('ctx', 'tp')
- grad_query: bfloat16 [4096, 2048], P('ctx', 'tp')
- grad_key: bfloat16 [4096, 512], P('ctx', 'tp')
- grad_value: bfloat16 [4096, 512], P('ctx', 'tp')
- grad_out: bfloat16 [4096, 2048], P('ctx', 'tp')
Inputs may be any that keep to these rules, and one draw needn't show every extreme that they name: `piece_doc`: every document has at least one piece; the pieces of one document, in increasing token order, have offsets 0, 8, 16 and so on. `piece_offset`: A piece belongs to the owner of its document. The pieces of the tokens of one index of ctx go to exactly 8 / 2 owners, exactly 128 tokens to each of them; so every owner receives 512 tokens. `doc_owner`: every device of ctx owns exactly 4 documents.
All inputs are finite; a program needn't handle non-finite values.
Results may differ from a plain program's by a relative error of at most 0.015.
Values may be sent and summed in bfloat16 or wider, within the bound.
A program may use at most 128 MiB of HBM per device.

v0:
```python
import functools
import math

import jax
import jax.numpy as jnp
from jax import lax
from jax.experimental import pallas as pl
from jax.experimental.pallas import tpu as pltpu
from jax.sharding import PartitionSpec as P

HEAD_SIZE = 128
PIECE = 8


rope_base = 500000.0
fill_value = -1e30


def apply_rotary(heads, positions, direction):
    half_width = heads.shape[-1] // 2
    frequency = rope_base ** (-2.0 * jnp.arange(half_width, dtype=jnp.float32) / heads.shape[-1])
    angles = positions.astype(jnp.float32)[:, None] * frequency[None, :]
    cosine = jnp.cos(angles)[:, None, :]
    sine_term = direction * jnp.sin(angles)[:, None, :]
    lower_half = heads[..., :half_width]
    upper_half = heads[..., half_width:]
    return jnp.concatenate(
        [
            lower_half * cosine - upper_half * sine_term,
            upper_half * cosine + lower_half * sine_term,
        ],
        axis=-1,
    )


def mask_of(query_doc, query_pos, key_doc, key_pos):
    return (query_doc[:, None] == key_doc[None, :]) & (key_pos[None, :] <= query_pos[:, None])


def attend_both(query_matrix, key_heads, value_heads, out_grads, allowed, score_scale):
    scores = (
        jnp.einsum("bkgd,mkd->kgbm", query_matrix, key_heads, preferred_element_type=jnp.float32)
        * score_scale
    )
    scores = jnp.where(allowed, scores, fill_value)
    row_max = jnp.max(scores, axis=-1, keepdims=True)
    exponent = jnp.where(allowed, jnp.exp(scores - row_max), 0.0)
    row_sum = jnp.sum(exponent, axis=-1, keepdims=True)
    probability = exponent / row_sum
    rounded = probability.astype(jnp.bfloat16)
    attended = jnp.einsum(
        "kgbm,mkd->bkgd", rounded, value_heads, preferred_element_type=jnp.float32
    ).astype(jnp.bfloat16)
    row_delta = jnp.einsum(
        "bkgd,bkgd->kgb", out_grads.astype(jnp.float32), attended.astype(jnp.float32)
    )
    prob_grad = jnp.einsum(
        "bkgd,mkd->kgbm", out_grads, value_heads, preferred_element_type=jnp.float32
    )
    score_grad = (probability * (prob_grad - row_delta[..., None])).astype(jnp.bfloat16)
    query_gradient = (
        jnp.einsum("kgbm,mkd->bkgd", score_grad, key_heads, preferred_element_type=jnp.float32)
        * score_scale
    )
    key_gradient = (
        jnp.einsum("kgbm,bkgd->mkd", score_grad, query_matrix, preferred_element_type=jnp.float32)
        * score_scale
    )
    value_gradient = jnp.einsum(
        "kgbm,bkgd->mkd", rounded, out_grads, preferred_element_type=jnp.float32
    )
    return attended, query_gradient, key_gradient, value_gradient


def contract_rows(left, right):
    return lax.dot_general(
        left, right, (((0,), (0,)), ((), ())), preferred_element_type=jnp.float32
    )


def contract_cols(left, right):
    return lax.dot_general(
        left, right, (((1,), (1,)), ((), ())), preferred_element_type=jnp.float32
    )


def spot_of(device, count):
    odd = lax.rem(device, 2)
    half = lax.div(device, 2)
    return (1 - odd) * half + odd * (count - 1 - half)


def device_at(spot, count):
    high = lax.div(spot, count // 2)
    return (1 - high) * (2 * spot) + high * (2 * (count - 1 - spot) + 1)


def sums_kernel(
    count,
    q_width,
    kv_width,
    input_t,
    cotangent_t,
    weights,
    gradients,
    attended,
    grad_in,
    grad_query,
    grad_key,
    grad_value,
    grad_out,
    ring0,
    ring1,
    ring2,
    ring3,
    near_sent,
    near_got,
    far_sent,
    far_got,
    ring_send,
    ring_recv,
    tp_send,
    tp_recv,
):
    me = lax.axis_index("ctx")
    tp = lax.axis_index("tp")
    here = spot_of(me, count)
    after = device_at(lax.rem(here + 1, count), count)
    before = device_at(lax.rem(here + count - 1, count), count)
    low_bit = lax.rem(tp, 2)
    high_bit = lax.div(tp, 2)
    near = tp + 1 - 2 * low_bit
    far = tp + 2 - 4 * high_bit
    mesh_id = pl.DeviceIdType.MESH
    barrier = pltpu.get_barrier_semaphore()
    for target in ((after, tp), (before, tp), (me, near), (me, far)):
        pl.semaphore_signal(barrier, inc=1, device_id=target, device_id_type=mesh_id)
    pl.semaphore_wait(barrier, 4)

    block_rows = input_t.shape[0] // count
    half_grad = gradients.shape[1] // 2
    half_out = attended.shape[1] // 2
    rings = (
        (ring0, input_t, gradients, 0, half_grad, 1),
        (ring1, input_t, gradients, half_grad, half_grad, -1),
        (ring2, cotangent_t, attended, 0, half_out, 1),
        (ring3, cotangent_t, attended, half_out, half_out, -1),
    )

    def term(ring, hop):
        _, left, right, start, width, step = rings[ring]
        if step > 0:
            spot = lax.rem(here + 2 * count - 1 - hop, count)
        else:
            spot = lax.rem(here + 1 + hop, count)
        row = pl.multiple_of(device_at(spot, count) * block_rows, block_rows)
        return jnp.dot(
            left[pl.ds(row, block_rows), :],
            right[:, start : start + width],
            preferred_element_type=jnp.float32,
        )

    def ring_copy(ring, hop):
        buffer = rings[ring][0]
        return pltpu.make_async_remote_copy(
            src_ref=buffer.at[hop],
            dst_ref=buffer.at[hop + 1],
            send_sem=ring_send.at[ring, hop],
            recv_sem=ring_recv.at[ring, hop],
            device_id=(after if rings[ring][5] > 0 else before, tp),
            device_id_type=mesh_id,
        )

    for ring in range(4):
        rings[ring][0][0] = term(ring, 0).astype(jnp.bfloat16)
        ring_copy(ring, 0).start()

    def input_term(chunk):
        rows = grad_in.shape[1]
        row = pl.multiple_of(chunk * rows, rows)
        return lax.dot_general(
            gradients[...],
            weights[pl.ds(row, rows), :],
            (((1,), (1,)), ((), ())),
            preferred_element_type=jnp.float32,
        )

    def near_copy(slot):
        return pltpu.make_async_remote_copy(
            src_ref=near_sent.at[slot],
            dst_ref=near_got.at[slot],
            send_sem=tp_send.at[slot],
            recv_sem=tp_recv.at[slot],
            device_id=(me, near),
            device_id_type=mesh_id,
        )

    far_copy = pltpu.make_async_remote_copy(
        src_ref=far_sent,
        dst_ref=far_got,
        send_sem=tp_send.at[2],
        recv_sem=tp_recv.at[2],
        device_id=(me, far),
        device_id_type=mesh_id,
    )

    near_sent[0] = input_term(2 * (1 - high_bit) + 1 - low_bit).astype(jnp.bfloat16)
    near_copy(0).start()
    near_sent[1] = input_term(2 * high_bit + 1 - low_bit).astype(jnp.bfloat16)
    near_copy(1).start()

    def ring_hop(hop, carry):
        for ring in range(4):
            ring_copy(ring, hop - 1).wait_recv()
            buffer = rings[ring][0]
            total = term(ring, hop) + buffer[hop].astype(jnp.float32)
            buffer[hop] = total.astype(jnp.bfloat16)
            ring_copy(ring, hop).start()
        return carry

    early = min(2, count - 1)
    lax.fori_loop(1, early, ring_hop, 0)
    near_copy(0).wait_recv()
    far_sent[...] = (
        input_term(2 * (1 - high_bit) + low_bit) + near_got[0].astype(jnp.float32)
    ).astype(jnp.bfloat16)
    far_copy.start()
    lax.fori_loop(early, count - 1, ring_hop, 0)

    near_copy(1).wait_recv()
    far_copy.wait_recv()
    grad_in[...] = (
        input_term(2 * high_bit + low_bit)
        + near_got[1].astype(jnp.float32)
        + far_got[...].astype(jnp.float32)
    ).astype(jnp.bfloat16)

    pieces = (
        (grad_query, 0, q_width),
        (grad_key, q_width, kv_width),
        (grad_value, q_width + kv_width, kv_width),
    )
    for ring in range(4):
        ring_copy(ring, count - 2).wait_recv()
        buffer, _, right, start, width, _ = rings[ring]
        total = term(ring, count - 1) + buffer[count - 1].astype(jnp.float32)
        total = total.astype(jnp.bfloat16)
        if right is attended:
            grad_out[:, start : start + width] = total
        else:
            for target, low, size in pieces:
                first, last = max(low, start), min(low + size, start + width)
                if first < last:
                    target[:, first - low : last - low] = total[:, first - start : last - start]

    def drain(hop, carry):
        for ring in range(4):
            ring_copy(ring, hop).wait_send()
        return carry

    lax.fori_loop(0, count - 1, drain, 0)
    near_copy(0).wait_send()
    near_copy(1).wait_send()
    far_copy.wait_send()


def sum_products(input_t, cotangent_t, weights, gradients, attended, count, q_width, kv_width):
    model_width, tok_rows = input_t.shape
    block_rows = model_width // count
    in_width = model_width // 4
    half_grad = gradients.shape[1] // 2
    half_out = attended.shape[1] // 2
    half = jnp.bfloat16
    flops = 2 * tok_rows * model_width * (2 * gradients.shape[1] + attended.shape[1])
    vmem = pl.BlockSpec(memory_space=pltpu.VMEM)
    return pl.pallas_call(
        functools.partial(sums_kernel, count, q_width, kv_width),
        out_shape=(
            jax.ShapeDtypeStruct((tok_rows, in_width), half),
            jax.ShapeDtypeStruct((block_rows, q_width), half),
            jax.ShapeDtypeStruct((block_rows, kv_width), half),
            jax.ShapeDtypeStruct((block_rows, kv_width), half),
            jax.ShapeDtypeStruct((block_rows, q_width), half),
        ),
        in_specs=[vmem] * 5,
        out_specs=(vmem,) * 5,
        scratch_shapes=[
            pltpu.VMEM((count, block_rows, half_grad), half),
            pltpu.VMEM((count, block_rows, half_grad), half),
            pltpu.VMEM((count, block_rows, half_out), half),
            pltpu.VMEM((count, block_rows, half_out), half),
            pltpu.VMEM((2, tok_rows, in_width), half),
            pltpu.VMEM((2, tok_rows, in_width), half),
            pltpu.VMEM((tok_rows, in_width), half),
            pltpu.VMEM((tok_rows, in_width), half),
            pltpu.SemaphoreType.DMA((4, count - 1)),
            pltpu.SemaphoreType.DMA((4, count - 1)),
            pltpu.SemaphoreType.DMA((3,)),
            pltpu.SemaphoreType.DMA((3,)),
        ],
        compiler_params=pltpu.CompilerParams(
            collective_id=0, has_side_effects=True, vmem_limit_bytes=56 * 1024 * 1024
        ),
        cost_estimate=pl.CostEstimate(
            flops=flops, bytes_accessed=30 * model_width * tok_rows, transcendentals=0
        ),
    )(input_t, cotangent_t, weights, gradients, attended)


def on_device(
    normed_input,
    w_query,
    key_weight,
    value_weight,
    output_weight,
    output_cotangent,
    piece_doc,
    piece_offset,
    doc_owner,
):
    sources = lax.axis_size("ctx")
    self_index = lax.axis_index("ctx")
    tok_rows = normed_input.shape[0]
    local_q = w_query.shape[1] // HEAD_SIZE
    local_kv = key_weight.shape[1] // HEAD_SIZE
    group_width = local_q // local_kv
    q_width = w_query.shape[1]
    kv_width = key_weight.shape[1]
    per_device = tok_rows // PIECE
    slot_rows = 2 * tok_rows // sources
    per_slot = slot_rows // PIECE
    owner_rows = sources * slot_rows
    score_scale = 1.0 / math.sqrt(HEAD_SIZE)
    within = jnp.arange(PIECE, dtype=jnp.int32)
    doc_ids = jnp.arange(doc_owner.shape[0], dtype=jnp.int32)
    piece_owner = jnp.sum(
        jnp.where(piece_doc[:, None] == doc_ids[None, :], doc_owner[None, :], 0), axis=1
    )
    own_owner = lax.dynamic_slice_in_dim(piece_owner, self_index * per_device, per_device)
    own_offset = lax.dynamic_slice_in_dim(piece_offset, self_index * per_device, per_device)
    own_pos = (own_offset[:, None] + within[None, :]).reshape(-1)
    piece_ids = jnp.arange(per_device, dtype=jnp.int32)
    earlier = (own_owner[:, None] == own_owner[None, :]) & (piece_ids[None, :] < piece_ids[:, None])
    own_rank = jnp.sum(earlier.astype(jnp.int32), axis=1)
    own_slot = own_owner * per_slot + own_rank
    own_row = (own_slot[:, None] * PIECE + within[None, :]).reshape(-1)
    placing = (jnp.arange(owner_rows, dtype=jnp.int32)[:, None] == own_row[None, :]).astype(
        jnp.bfloat16
    )

    def to_slots(matrix):
        return jnp.dot(placing, matrix, preferred_element_type=jnp.float32).astype(jnp.bfloat16)

    def from_slots(matrix):
        return contract_rows(placing, matrix).astype(jnp.bfloat16)

    def exchange(matrix):
        return lax.all_to_all(matrix, "ctx", split_axis=0, concat_axis=0, tiled=True)

    grad_rows = jnp.dot(output_cotangent, output_weight, preferred_element_type=jnp.float32).astype(
        jnp.bfloat16
    )
    got_grad = exchange(to_slots(grad_rows))
    query_rows = apply_rotary(
        jnp.dot(normed_input, w_query, preferred_element_type=jnp.float32).reshape(
            tok_rows, local_q, HEAD_SIZE
        ),
        own_pos,
        1.0,
    )
    query_rows = query_rows.astype(jnp.bfloat16).reshape(tok_rows, q_width)
    got_query = exchange(to_slots(query_rows))
    all_ids = jnp.arange(piece_owner.shape[0], dtype=jnp.int32)
    mine = piece_owner == self_index
    preceding = mine[None, :] & (all_ids[None, :] < all_ids[:, None])
    same_source = (all_ids[None, :] // per_device) == (all_ids[:, None] // per_device)
    live_rank = jnp.sum(preceding.astype(jnp.int32), axis=1)
    source_rank = jnp.sum((preceding & same_source).astype(jnp.int32), axis=1)
    choosing = mine[None, :] & (live_rank[None, :] == piece_ids[:, None])

    def choose(table):
        return jnp.sum(jnp.where(choosing, table[None, :], 0), axis=1)

    compact_slot = choose(all_ids // per_device * per_slot + source_rank)
    compact_row = (compact_slot[:, None] * PIECE + within[None, :]).reshape(-1)
    packing = (
        jnp.arange(owner_rows, dtype=jnp.int32)[None, :] == compact_row[:, None]
    ).astype(jnp.bfloat16)
    row_doc = jnp.repeat(choose(piece_doc), PIECE)
    row_pos = (choose(piece_offset)[:, None] + within[None, :]).reshape(-1)
    pair_weights = jnp.concatenate([key_weight, value_weight], axis=1)
    weights = jnp.concatenate([w_query, pair_weights], axis=1)
    input_t = normed_input.T
    cotangent_t = output_cotangent.T
    packing, row_doc, row_pos, pair_weights, normed_input = lax.optimization_barrier(
        (packing, row_doc, row_pos, pair_weights, normed_input)
    )
    pair_rows = jnp.dot(normed_input, pair_weights, preferred_element_type=jnp.float32)
    key_rows = apply_rotary(
        pair_rows[:, :kv_width].reshape(tok_rows, local_kv, HEAD_SIZE), own_pos, 1.0
    )
    key_rows = key_rows.reshape(tok_rows, kv_width)
    pair_rows = jnp.concatenate([key_rows, pair_rows[:, kv_width:]], axis=1).astype(jnp.bfloat16)
    got_pair = exchange(to_slots(pair_rows))

    def to_live(matrix):
        return jnp.dot(packing, matrix, preferred_element_type=jnp.float32).astype(jnp.bfloat16)

    def to_owner_slots(matrix):
        return contract_rows(packing, matrix).astype(jnp.bfloat16)

    live_pair = to_live(got_pair)
    attended, query_gradient, key_gradient, value_gradient = attend_both(
        to_live(got_query).reshape(tok_rows, local_kv, group_width, HEAD_SIZE),
        live_pair[:, :kv_width].reshape(tok_rows, local_kv, HEAD_SIZE),
        live_pair[:, kv_width:].reshape(tok_rows, local_kv, HEAD_SIZE),
        to_live(got_grad).reshape(tok_rows, local_kv, group_width, HEAD_SIZE),
        mask_of(row_doc, row_pos, row_doc, row_pos),
        score_scale,
    )
    back_attended = exchange(to_owner_slots(attended.reshape(tok_rows, q_width)))
    query_gradient = apply_rotary(
        query_gradient.reshape(tok_rows, local_q, HEAD_SIZE), row_pos, -1.0
    )
    key_gradient = apply_rotary(key_gradient, row_pos, -1.0)
    gradients = jnp.concatenate(
        [
            query_gradient.reshape(tok_rows, q_width),
            key_gradient.reshape(tok_rows, kv_width),
            value_gradient.reshape(tok_rows, kv_width),
        ],
        axis=1,
    ).astype(jnp.bfloat16)
    back_gradients = exchange(to_owner_slots(gradients))
    local_attended = from_slots(back_attended)
    local_gradients = from_slots(back_gradients)

    return sum_products(
        input_t,
        cotangent_t,
        weights,
        local_gradients,
        local_attended,
        sources,
        q_width,
        kv_width,
    )


def solution(mesh):
    return jax.shard_map(
        on_device,
        mesh=mesh,
        in_specs=(
            P("ctx", None),
            P(None, "tp"),
            P(None, "tp"),
            P(None, "tp"),
            P(None, "tp"),
            P("ctx", None),
            P(),
            P(),
            P(),
        ),
        out_specs=(P("ctx", "tp"), P("ctx", "tp"), P("ctx", "tp"), P("ctx", "tp"), P("ctx", "tp")),
        check_vma=False,
    )
```

profile of v0, /device:TPU:0, one launch (start us, length us, event | category | flops | bytes accessed | tf_op | source)
XLA Modules:
  0.0 296.8 jit_solution(9732420363761537567)
XLA Ops:
  0.7 0.8 select_reduce_fusion.3
  1.5 0.8 dynamic_slice.7
  2.6 0.9 select_reduce_fusion
  4.3 1.9 pad_maximum_fusion.1
  6.2 0.6 copy-done.2
  6.8 1.3 fusion.96
  9.4 1.3 fusion.30
  10.7 7.3 %all-to-all-start = ((bf16[8,128,256]{2,1,0:T(8,128)(2,1)}), bf16[8,128,256]{2,1,0:T(8,128)(2,1)S(1)}, u32[]{:S(2)}, u32[]{:S(2)}) async-start(bf16[8,128,256]{2,1,0:T(8,128)(2,1)} %bitcast.6), calls=%async_computation | async-start | bytes 1048576 | tf_op jit(solution)/shard_map/all_to_all | solution.py:358
  18.0 7.4 %fusion.21 = bf16[1024,512]{1,0:T(8,128)(2,1)} fusion(s32[512]{0:T(512)S(1)} %add.123, bf16[512,4096]{1,0:T(8,128)(2,1)} %param.14, bf16[4096,512]{1,0:T(8,128)(2,1)} %param.13), kind=kOutput, calls=%fused_computation.29 | convolution fusion | flops 2685665280 | bytes 9439232 | tf_op jit(solution)/shard_map/dot_general | solution.py:352
  25.3 7.1 %all-to-all-done = bf16[8,128,256]{2,1,0:T(8,128)(2,1)S(1)} async-done(((bf16[8,128,256]{2,1,0:T(8,128)(2,1)}), bf16[8,128,256]{2,1,0:T(8,128)(2,1)S(1)}, u32[]{:S(2)}, u32[]{:S(2)}) %all-to-all-start) | async-done | bytes 524320 | tf_op jit(solution)/shard_map/all_to_all | solution.py:358
  32.4 0.8 copy-done.5
  33.2 3.6 %all-to-all-start.2 = ((bf16[8,128,512]{2,1,0:T(8,128)(2,1)}), bf16[8,128,512]{2,1,0:T(8,128)(2,1)S(1)}, u32[]{:S(2)}, u32[]{:S(2)}) async-start(bf16[8,128,512]{2,1,0:T(8,128)(2,1)} %bitcast.18), calls=%async_computation.2 | async-start | bytes 2097152 | tf_op jit(solution)/shard_map/all_to_all | solution.py:358
  36.9 1.7 multiply_cosine_fusion.1
  38.6 5.8 %fusion.97 = f32[512,512]{0,1:T(8,128)S(1)} fusion(bf16[512,4096]{1,0:T(8,128)(2,1)} %param.9, bf16[4096,512]{1,0:T(8,128)(2,1)} %param.10), kind=kOutput, calls=%fused_computation.136 | convolution fusion | flops 2147483648 | bytes 9437184 | tf_op jit(solution)/shard_map/dot_general | solution.py:365
  44.7 1.7 fusion.20
  46.4 16.4 %all-to-all-done.2 = bf16[8,128,512]{2,1,0:T(8,128)(2,1)S(1)} async-done(((bf16[8,128,512]{2,1,0:T(8,128)(2,1)}), bf16[8,128,512]{2,1,0:T(8,128)(2,1)S(1)}, u32[]{:S(2)}, u32[]{:S(2)}) %all-to-all-start.2) | async-done | bytes 1048608 | tf_op jit(solution)/shard_map/all_to_all | solution.py:358
  62.8 3.7 %all-to-all-start.1 = ((bf16[8,128,512]{2,1,0:T(8,128)(2,1)}), bf16[8,128,512]{2,1,0:T(8,128)(2,1)S(1)}, u32[]{:S(2)}, u32[]{:S(2)}) async-start(bf16[8,128,512]{2,1,0:T(8,128)(2,1)} %bitcast.12), calls=%async_computation.1 | async-start | bytes 2097152 | tf_op jit(solution)/shard_map/all_to_all | solution.py:358
  66.8 2.2 convolution_convert_fusion.5
  69.0 1.6 convolution_convert_fusion.3
  70.6 21.8 %all-to-all-done.1 = bf16[8,128,512]{2,1,0:T(8,128)(2,1)S(1)} async-done(((bf16[8,128,512]{2,1,0:T(8,128)(2,1)}), bf16[8,128,512]{2,1,0:T(8,128)(2,1)S(1)}, u32[]{:S(2)}, u32[]{:S(2)}) %all-to-all-start.1) | async-done | bytes 1048608 | tf_op jit(solution)/shard_map/all_to_all | solution.py:358
  92.4 0.8 convolution_convert_fusion.4
  93.2 1.8 fusion.2
  95.1 1.0 fusion.4
  96.1 1.6 fusion.52
  97.8 1.8 fusion.1
  99.5 0.8 fusion.43
  100.4 1.2 fusion.75
  101.6 1.7 convolution_convert_fusion.1
  103.3 4.4 %all-to-all-start.4 = ((bf16[8,128,512]{2,1,0:T(8,128)(2,1)}), bf16[8,128,512]{2,1,0:T(8,128)(2,1)}, u32[]{:S(2)}, u32[]{:S(2)}) async-start(bf16[8,128,512]{2,1,0:T(8,128)(2,1)} %bitcast.168), calls=%async_computation.4 | async-start | bytes 2097152 | tf_op jit(solution)/shard_map/all_to_all | solution.py:358
  107.7 1.0 maximum_bitcast_fusion.1
  108.7 1.8 fusion.26
  110.5 1.1 subtract_convert_fusion
  111.7 1.5 fusion.49
  113.2 2.2 convolution_convert_fusion
  115.4 17.9 %all-to-all-done.4 = bf16[8,128,512]{2,1,0:T(8,128)(2,1)} async-done(((bf16[8,128,512]{2,1,0:T(8,128)(2,1)}), bf16[8,128,512]{2,1,0:T(8,128)(2,1)}, u32[]{:S(2)}, u32[]{:S(2)}) %all-to-all-start.4) | async-done | bytes 1048608 | tf_op jit(solution)/shard_map/all_to_all | solution.py:358
  133.3 4.5 %all-to-all-start.3 = ((bf16[8,128,768]{2,1,0:T(8,128)(2,1)}), bf16[8,128,768]{2,1,0:T(8,128)(2,1)}, u32[]{:S(2)}, u32[]{:S(2)}) async-start(bf16[8,128,768]{2,1,0:T(8,128)(2,1)} %bitcast.48), calls=%async_computation.3 | async-start | bytes 3145728 | tf_op jit(solution)/shard_map/all_to_all | solution.py:358
  137.8 6.5 %copy.35 = bf16[512,4096]{0,1:T(8,128)(2,1)} copy(bf16[512,4096]{1,0:T(8,128)(2,1)} %param.14) | data formatting | bytes 8388608 | tf_op args[5]
  144.3 6.7 %copy.34 = bf16[512,4096]{0,1:T(8,128)(2,1)} copy(bf16[512,4096]{1,0:T(8,128)(2,1)} %param.9) | data formatting | bytes 8388608 | tf_op args[0]
  151.0 5.5 %pad_maximum_fusion.weights = bf16[4096,768]{1,0:T(8,128)(2,1)} fusion(bf16[4096,128]{1,0:T(8,128)(2,1)S(1)} %copy-done.3, bf16[4096,128]{1,0:T(8,128)(2,1)S(1)} %copy-done.4, bf16[4096,512]{1,0:T(8,128)(2,1)} %param.10), kind=kLoop, calls=%fused_computation | loop fusion | flops 18874368 | bytes 12582912 | tf_op jit(solution)/shard_map/concatenate | solution.py:392
  156.5 2.8 fusion.29.attended
  159.3 15.0 %all-to-all-done.3 = bf16[8,128,768]{2,1,0:T(8,128)(2,1)} async-done(((bf16[8,128,768]{2,1,0:T(8,128)(2,1)}), bf16[8,128,768]{2,1,0:T(8,128)(2,1)}, u32[]{:S(2)}, u32[]{:S(2)}) %all-to-all-start.3) | async-done | bytes 1572896 | tf_op jit(solution)/shard_map/all_to_all | solution.py:358
  174.2 3.5 %fusion.22.gradients = bf16[512,768]{1,0:T(8,128)(2,1)} fusion(bf16[1024,768]{1,0:T(8,128)(2,1)} %bitcast.49, s32[512]{0:T(512)S(1)} %copy-done.10), kind=kOutput, calls=%fused_computation.31 | convolution fusion | flops 806223872 | bytes 2361344 | tf_op jit(solution)/shard_map/dot_general | solution.py:76
  177.7 109.9 %shard_map.128 = (bf16[512,1024]{1,0:T(8,128)(2,1)}, bf16[512,512]{1,0:T(8,128)(2,1)}, bf16[512,128]{1,0:T(8,128)(2,1)}, bf16[512,128]{1,0:T(8,128)(2,1)}, bf16[512,512]{1,0:T(8,128)(2,1)}) custom-call(bf16[4096,512]{1,0:T(8,128)(2,1)} %bitcast.163, bf16[4096,512]{1,0:T(8,128)(2,1)} %bitcast.162, bf16[4096,768]{1,0:T(8,128)(2,1)} %pad_maximum_fusion.weights, ...), custom_call_target="tpu_custom_call" | custom-call | flops 8589934592 | bytes 62914560 | tf_op jit(solution)/shard_map/pallas_call | solution.py:276
  287.7 2.3 copy.66
  289.9 1.9 copy.67
  291.8 1.6 copy.68
  293.4 1.6 copy.69
  294.9 1.9 copy.70
  (53 shorter events, 3.0 us)
Async XLA Ops:
  4.0 2.8 copy-start.2
  8.6 36.0 %copy-start.9 = (s32[512]{0:T(512)}, s32[512]{0:T(512)S(1)}, u32[]{:S(2)}) copy-start(s32[512]{0:T(512)S(1)} %add.123) | copy-start | bytes 6148
  10.7 21.7 %all-to-all-start = ((bf16[8,128,256]{2,1,0:T(8,128)(2,1)}), bf16[8,128,256]{2,1,0:T(8,128)(2,1)S(1)}, u32[]{:S(2)}, u32[]{:S(2)}) async-start(bf16[8,128,256]{2,1,0:T(8,128)(2,1)} %bitcast.6), calls=%async_computation | async-start | bytes 1048576 | tf_op jit(solution)/shard_map/all_to_all | solution.py:358
  32.4 0.8 copy-start.5
  33.2 29.6 %all-to-all-start.2 = ((bf16[8,128,512]{2,1,0:T(8,128)(2,1)}), bf16[8,128,512]{2,1,0:T(8,128)(2,1)S(1)}, u32[]{:S(2)}, u32[]{:S(2)}) async-start(bf16[8,128,512]{2,1,0:T(8,128)(2,1)} %bitcast.18), calls=%async_computation.2 | async-start | bytes 2097152 | tf_op jit(solution)/shard_map/all_to_all | solution.py:358
  62.8 29.6 %all-to-all-start.1 = ((bf16[8,128,512]{2,1,0:T(8,128)(2,1)}), bf16[8,128,512]{2,1,0:T(8,128)(2,1)S(1)}, u32[]{:S(2)}, u32[]{:S(2)}) async-start(bf16[8,128,512]{2,1,0:T(8,128)(2,1)} %bitcast.12), calls=%async_computation.1 | async-start | bytes 2097152 | tf_op jit(solution)/shard_map/all_to_all | solution.py:358
  93.2 2.9 copy-start.6
  93.2 2.9 copy-start.11
  95.0 2.7 copy-start
  96.1 1.6 copy-start.7
  103.3 8.4 %copy-start.8 = (f32[4,512]{1,0:T(4,128)S(1)}, f32[4,512]{1,0:T(4,128)}, u32[]{:S(2)}) copy-start(f32[4,512]{1,0:T(4,128)} %copy-done.7) | copy-start | bytes 24580
  103.3 30.0 %all-to-all-start.4 = ((bf16[8,128,512]{2,1,0:T(8,128)(2,1)}), bf16[8,128,512]{2,1,0:T(8,128)(2,1)}, u32[]{:S(2)}, u32[]{:S(2)}) async-start(bf16[8,128,512]{2,1,0:T(8,128)(2,1)} %bitcast.168), calls=%async_computation.4 | async-start | bytes 2097152 | tf_op jit(solution)/shard_map/all_to_all | solution.py:358
  107.7 4.0 %copy-start.1 = (f32[512,512,4]{1,0,2:T(8,128)S(1)}, f32[512,512,4]{1,0,2:T(8,128)}, u32[]{:S(2)}) copy-start(f32[512,512,4]{1,0,2:T(8,128)} %copy-done) | copy-start | bytes 12582916
  107.7 4.0 %copy-start.12 = (bf16[512,512]{0,1:T(8,128)(2,1)S(1)}, bf16[512,512]{0,1:T(8,128)(2,1)}, u32[]{:S(2)}) copy-start(bf16[512,512]{0,1:T(8,128)(2,1)} %convolution_convert_fusion.3) | copy-start | bytes 1572868
  133.3 40.9 %all-to-all-start.3 = ((bf16[8,128,768]{2,1,0:T(8,128)(2,1)}), bf16[8,128,768]{2,1,0:T(8,128)(2,1)}, u32[]{:S(2)}, u32[]{:S(2)}) async-start(bf16[8,128,768]{2,1,0:T(8,128)(2,1)} %bitcast.48), calls=%async_computation.3 | async-start | bytes 3145728 | tf_op jit(solution)/shard_map/all_to_all | solution.py:358
  144.3 6.7 %copy-start.3 = (bf16[4096,128]{1,0:T(8,128)(2,1)S(1)}, bf16[4096,128]{1,0:T(8,128)(2,1)}, u32[]{:S(2)}) copy-start(bf16[4096,128]{1,0:T(8,128)(2,1)} %param.12) | copy-start | bytes 3145732
  144.3 6.7 %copy-start.4 = (bf16[4096,128]{1,0:T(8,128)(2,1)S(1)}, bf16[4096,128]{1,0:T(8,128)(2,1)}, u32[]{:S(2)}) copy-start(bf16[4096,128]{1,0:T(8,128)(2,1)} %param.11) | copy-start | bytes 3145732
  151.0 5.5 %copy-start.10 = (s32[512]{0:T(512)S(1)}, s32[512]{0:T(512)}, u32[]{:S(2)}) copy-start(s32[512]{0:T(512)} %copy-done.9) | copy-start | bytes 6148
where the time goes:
time: 298 us; the launch traced here: 297 us
  Pallas kernels  110 us (37%)
  waiting for transfers between devices  78.2 us (26%)
  matrix products  41.5 us (14%)
  local copies, waits for them, and re-layouts  25.2 us (8%)
  starting transfers between devices  23.5 us (8%)
  other arithmetic  17.4 us (6%)
    pallas_call x1, Pallas kernels, sum_products(): pl.pallas_call(functools.partial(sums_kernel, count, q_width, kv_width),...  110 us
    all_to_all x5, waiting for transfers between devices, exchange(): lax.all_to_all(matrix, 'ctx', split_axis=0, concat_axis=0, tiled=True)  78.2 us
    unnamed x33, local copies, waits for them, and re-layouts  23.8 us
    all_to_all x5, starting transfers between devices, exchange(): lax.all_to_all(matrix, 'ctx', split_axis=0, concat_axis=0, tiled=True)  23.5 us
    dot_general x3, matrix products, to_slots(): jnp.dot(placing, matrix, preferred_element_type=jnp.float32)  10.4 us
    dot_general x4, matrix products, contract_rows(): lax.dot_general(left, right, (((0,), (0,)), ((), ())), preferred_element_...  10.2 us
  transfers between devices with their start and end apart: 5, of which 5 were waited for; matrix products, arithmetic and copies ran while one was open for 17% of the time, Pallas kernels for 0%

commit v1 on v0

--- a/solution.py
+++ b/solution.py
@@ -211,9 +211,10 @@
 
     def ring_hop(hop, carry):
         for ring in range(4):
+            product = term(ring, hop)
             ring_copy(ring, hop - 1).wait_recv()
             buffer = rings[ring][0]
-            total = term(ring, hop) + buffer[hop].astype(jnp.float32)
+            total = product + buffer[hop].astype(jnp.float32)
             buffer[hop] = total.astype(jnp.bfloat16)
             ring_copy(ring, hop).start()
         return carry
@@ -369,7 +370,6 @@
         1.0,
     )
     query_rows = query_rows.astype(jnp.bfloat16).reshape(tok_rows, q_width)
-    got_query = exchange(to_slots(query_rows))
     all_ids = jnp.arange(piece_owner.shape[0], dtype=jnp.int32)
     mine = piece_owner == self_index
     preceding = mine[None, :] & (all_ids[None, :] < all_ids[:, None])
@@ -392,16 +392,20 @@
     weights = jnp.concatenate([w_query, pair_weights], axis=1)
     input_t = normed_input.T
     cotangent_t = output_cotangent.T
-    packing, row_doc, row_pos, pair_weights, normed_input = lax.optimization_barrier(
-        (packing, row_doc, row_pos, pair_weights, normed_input)
-    )
     pair_rows = jnp.dot(normed_input, pair_weights, preferred_element_type=jnp.float32)
     key_rows = apply_rotary(
         pair_rows[:, :kv_width].reshape(tok_rows, local_kv, HEAD_SIZE), own_pos, 1.0
     )
     key_rows = key_rows.reshape(tok_rows, kv_width)
-    pair_rows = jnp.concatenate([key_rows, pair_rows[:, kv_width:]], axis=1).astype(jnp.bfloat16)
-    got_pair = exchange(to_slots(pair_rows))
+    sent_rows = jnp.concatenate(
+        [
+            query_rows,
+            key_rows.astype(jnp.bfloat16),
+            pair_rows[:, kv_width:].astype(jnp.bfloat16),
+        ],
+        axis=1,
+    )
+    got_rows = exchange(to_slots(sent_rows))
 
     def to_live(matrix):
         return jnp.dot(packing, matrix, preferred_element_type=jnp.float32).astype(jnp.bfloat16)
@@ -409,11 +413,11 @@
     def to_owner_slots(matrix):
         return contract_rows(packing, matrix).astype(jnp.bfloat16)
 
-    live_pair = to_live(got_pair)
+    live_rows = to_live(got_rows)
     attended, query_gradient, key_gradient, value_gradient = attend_both(
-        to_live(got_query).reshape(tok_rows, local_kv, group_width, HEAD_SIZE),
-        live_pair[:, :kv_width].reshape(tok_rows, local_kv, HEAD_SIZE),
-        live_pair[:, kv_width:].reshape(tok_rows, local_kv, HEAD_SIZE),
+        live_rows[:, :q_width].reshape(tok_rows, local_kv, group_width, HEAD_SIZE),
+        live_rows[:, q_width : q_width + kv_width].reshape(tok_rows, local_kv, HEAD_SIZE),
+        live_rows[:, q_width + kv_width :].reshape(tok_rows, local_kv, HEAD_SIZE),
         to_live(got_grad).reshape(tok_rows, local_kv, group_width, HEAD_SIZE),
         mask_of(row_doc, row_pos, row_doc, row_pos),
         score_scale,

time: 298 us -> 290 us (0.973)
  starting transfers between devices: 23.5 us -> 18.5 us
    all_to_all x5 -> x4, starting transfers between devices: 23.5 us -> 18.5 us  [exchange(): lax.all_to_all(matrix, 'ctx', split_axis=0, concat_axis=0, tiled=True)]
    all_to_all x5 -> x4, waiting for transfers between devices: 78.2 us -> 79.7 us  [exchange(): lax.all_to_all(matrix, 'ctx', split_axis=0, concat_axis=0, tiled=True)]
    dot_general x3 -> x2, matrix products: 10.4 us -> 9.71 us  [to_slots(): jnp.dot(placing, matrix, preferred_element_type=jnp.float32)]
    unnamed x33 -> x45, local copies, waits for them, and re-layouts: 23.8 us -> 23.2 us
  transfers between devices with their start and end apart: 5 -> 4, of which waited for: 5 -> 4; matrix products, arithmetic and copies ran while one was open for 17% -> 16% of each run, Pallas kernels for 0% -> 0%
where the time goes in v1:
time: 290 us; the launch traced here: 289 us
  Pallas kernels  110 us (38%)
  waiting for transfers between devices  79.7 us (27%)
  matrix products  40.9 us (14%)
  local copies, waits for them, and re-layouts  24.2 us (8%)
  starting transfers between devices  18.5 us (6%)
  other arithmetic  15.2 us (5%)
    pallas_call x1, Pallas kernels, sum_products(): pl.pallas_call(functools.partial(sums_kernel, count, q_width, kv_width),...  110 us
    all_to_all x4, waiting for transfers between devices, exchange(): lax.all_to_all(matrix, 'ctx', split_axis=0, concat_axis=0, tiled=True)  79.7 us
    unnamed x45, local copies, waits for them, and re-layouts  23.2 us
    all_to_all x4, starting transfers between devices, exchange(): lax.all_to_all(matrix, 'ctx', split_axis=0, concat_axis=0, tiled=True)  18.5 us
    dot_general x2, matrix products, to_slots(): jnp.dot(placing, matrix, preferred_element_type=jnp.float32)  9.71 us
    dot_general x4, matrix products, contract_rows(): lax.dot_general(left, right, (((0,), (0,)), ((), ())), preferred_element_...  7.85 us
    concatenate x1, other arithmetic, on_device(): weights = jnp.concatenate([w_query, pair_weights], axis=1)  6.09 us
    dot_general x1, matrix products, on_device(): jnp.dot(normed_input, w_query, preferred_element_type=jnp.float32)  5.83 us
  transfers between devices with their start and end apart: 4, of which 4 were waited for; matrix products, arithmetic and copies ran while one was open for 16% of the time, Pallas kernels for 0%

profile of v1, /device:TPU:0, one launch (start us, length us, event | category | flops | bytes accessed | tf_op | source)
XLA Modules:
  0.0 289.5 jit_solution(8170140850157549104)
XLA Ops:
  0.6 0.8 select_reduce_fusion.3
  1.5 0.2 convert_reduce_fusion.2
  1.8 0.1 add.134
  2.0 7.5 %fusion.26 = bf16[1024,512]{1,0:T(8,128)(2,1)} fusion(s32[512]{0:T(512)S(1)} %add.134, bf16[512,4096]{1,0:T(8,128)(2,1)} %param.14, bf16[4096,512]{1,0:T(8,128)(2,1)} %param.13), kind=kOutput, calls=%fused_computation.33 | convolution fusion | flops 2685665280 | bytes 9439232 | tf_op jit(solution)/shard_map/dot_general | solution.py:353
  9.5 7.3 %all-to-all-start.1 = ((bf16[8,128,512]{2,1,0:T(8,128)(2,1)}), bf16[8,128,512]{2,1,0:T(8,128)(2,1)S(1)}, u32[]{:S(2)}, u32[]{:S(2)}) async-start(bf16[8,128,512]{2,1,0:T(8,128)(2,1)} %bitcast.162), calls=%async_computation.1 | async-start | bytes 2097152 | tf_op jit(solution)/shard_map/all_to_all | solution.py:359
  16.8 3.5 %fusion.42 = f32[512,256]{0,1:T(8,128)S(1)} fusion(bf16[512,4096]{1,0:T(8,128)(2,1)} %param.9, bf16[4096,128]{1,0:T(8,128)(2,1)S(1)} %copy-done.2, bf16[4096,128]{1,0:T(8,128)(2,1)S(1)} %copy-done.4), kind=kOutput, calls=%fused_computation.43 | convolution fusion | flops 1077936128 | bytes 6815744 | tf_op jit(solution)/shard_map/dot_general | solution.py:395
  20.5 0.3 convert_reduce_fusion.1
  21.0 0.2 select_reduce_fusion.1
  21.3 0.6 fusion.95
  21.9 1.7 multiply_cosine_fusion.1
  23.6 5.8 %fusion.113 = f32[512,512]{0,1:T(8,128)S(1)} fusion(bf16[512,4096]{1,0:T(8,128)(2,1)} %param.9, bf16[4096,512]{1,0:T(8,128)(2,1)} %param.10), kind=kOutput, calls=%fused_computation.144 | convolution fusion | flops 2147483648 | bytes 9437184 | tf_op jit(solution)/shard_map/dot_general | solution.py:366
  29.5 0.2 subtract_convert_fusion.1
  29.7 2.2 fusion.25
  31.9 10.6 %all-to-all-done.1 = bf16[8,128,512]{2,1,0:T(8,128)(2,1)S(1)} async-done(((bf16[8,128,512]{2,1,0:T(8,128)(2,1)}), bf16[8,128,512]{2,1,0:T(8,128)(2,1)S(1)}, u32[]{:S(2)}, u32[]{:S(2)}) %all-to-all-start.1) | async-done | bytes 1048608 | tf_op jit(solution)/shard_map/all_to_all | solution.py:359
  42.5 3.8 %all-to-all-start = ((bf16[8,128,768]{2,1,0:T(8,128)(2,1)}), bf16[8,128,768]{2,1,0:T(8,128)(2,1)S(1)}, u32[]{:S(2)}, u32[]{:S(2)}) async-start(bf16[8,128,768]{2,1,0:T(8,128)(2,1)} %bitcast.9), calls=%async_computation | async-start | bytes 3145728 | tf_op jit(solution)/shard_map/all_to_all | solution.py:359
  46.6 0.3 compare_and_fusion
  46.9 1.7 fusion.38
  48.6 34.7 %all-to-all-done = bf16[8,128,768]{2,1,0:T(8,128)(2,1)S(1)} async-done(((bf16[8,128,768]{2,1,0:T(8,128)(2,1)}), bf16[8,128,768]{2,1,0:T(8,128)(2,1)S(1)}, u32[]{:S(2)}, u32[]{:S(2)}) %all-to-all-start) | async-done | bytes 1572896 | tf_op jit(solution)/shard_map/all_to_all | solution.py:359
  83.3 1.1 fusion.30
  84.4 0.9 copy-done.7
  85.3 0.2 copy.63
  85.6 1.8 fusion.2
  87.4 1.0 fusion.4
  88.5 2.7 fusion.63
  91.2 2.7 fusion.1
  93.9 0.8 fusion.54
  94.7 1.2 fusion.91
  95.9 1.9 convolution_convert_fusion.1
  97.8 3.7 %all-to-all-start.3 = ((bf16[8,128,512]{2,1,0:T(8,128)(2,1)}), bf16[8,128,512]{2,1,0:T(8,128)(2,1)S(1)}, u32[]{:S(2)}, u32[]{:S(2)}) async-start(bf16[8,128,512]{2,1,0:T(8,128)(2,1)} %bitcast.164), calls=%async_computation.3 | async-start | bytes 2097152 | tf_op jit(solution)/shard_map/all_to_all | solution.py:359
  101.5 1.0 maximum_bitcast_fusion.1
  102.6 1.8 fusion.34
  104.4 1.1 subtract_convert_fusion
  105.5 1.5 fusion.60
  107.1 2.3 convolution_convert_fusion
  109.4 18.1 %all-to-all-done.3 = bf16[8,128,512]{2,1,0:T(8,128)(2,1)S(1)} async-done(((bf16[8,128,512]{2,1,0:T(8,128)(2,1)}), bf16[8,128,512]{2,1,0:T(8,128)(2,1)S(1)}, u32[]{:S(2)}, u32[]{:S(2)}) %all-to-all-start.3) | async-done | bytes 1048608 | tf_op jit(solution)/shard_map/all_to_all | solution.py:359
  127.5 3.8 %all-to-all-start.2 = ((bf16[8,128,768]{2,1,0:T(8,128)(2,1)}), bf16[8,128,768]{2,1,0:T(8,128)(2,1)S(1)}, u32[]{:S(2)}, u32[]{:S(2)}) async-start(bf16[8,128,768]{2,1,0:T(8,128)(2,1)} %bitcast.46), calls=%async_computation.2 | async-start | bytes 3145728 | tf_op jit(solution)/shard_map/all_to_all | solution.py:359
  131.3 6.5 %copy.37 = bf16[512,4096]{0,1:T(8,128)(2,1)} copy(bf16[512,4096]{1,0:T(8,128)(2,1)} %param.14) | data formatting | bytes 8388608 | tf_op args[5]
  137.8 6.6 %copy.36 = bf16[512,4096]{0,1:T(8,128)(2,1)} copy(bf16[512,4096]{1,0:T(8,128)(2,1)} %param.9) | data formatting | bytes 8388608 | tf_op args[0]
  144.5 6.1 %pad_maximum_fusion.weights = bf16[4096,768]{1,0:T(8,128)(2,1)} fusion(bf16[4096,128]{1,0:T(8,128)(2,1)S(1)} %copy-done.3, bf16[4096,128]{1,0:T(8,128)(2,1)} %param.11, bf16[4096,512]{1,0:T(8,128)(2,1)} %param.10), kind=kLoop, calls=%fused_computation | loop fusion | flops 18874368 | bytes 12582912 | tf_op jit(solution)/shard_map/concatenate | solution.py:392
  150.5 1.6 fusion.37.attended
  152.1 16.3 %all-to-all-done.2 = bf16[8,128,768]{2,1,0:T(8,128)(2,1)S(1)} async-done(((bf16[8,128,768]{2,1,0:T(8,128)(2,1)}), bf16[8,128,768]{2,1,0:T(8,128)(2,1)S(1)}, u32[]{:S(2)}, u32[]{:S(2)}) %all-to-all-start.2) | async-done | bytes 1572896 | tf_op jit(solution)/shard_map/all_to_all | solution.py:359
  168.4 2.1 fusion.29.gradients
  170.5 109.9 %shard_map.128 = (bf16[512,1024]{1,0:T(8,128)(2,1)}, bf16[512,512]{1,0:T(8,128)(2,1)}, bf16[512,128]{1,0:T(8,128)(2,1)}, bf16[512,128]{1,0:T(8,128)(2,1)}, bf16[512,512]{1,0:T(8,128)(2,1)}) custom-call(bf16[4096,512]{1,0:T(8,128)(2,1)} %bitcast.157, bf16[4096,512]{1,0:T(8,128)(2,1)} %bitcast.156, bf16[4096,768]{1,0:T(8,128)(2,1)} %pad_maximum_fusion.weights, ...), custom_call_target="tpu_custom_call" | custom-call | flops 8589934592 | bytes 62914560 | tf_op jit(solution)/shard_map/pallas_call | solution.py:277
  280.4 2.3 copy.69
  282.6 1.9 copy.70
  284.5 1.6 copy.71
  286.1 1.6 copy.72
  287.6 1.9 copy.73
  (61 shorter events, 1.3 us)
Async XLA Ops:
  1.9 7.5 %copy-start.12 = (s32[512]{0:T(512)}, s32[512]{0:T(512)S(1)}, u32[]{:S(2)}) copy-start(s32[512]{0:T(512)S(1)} %add.134) | copy-start | bytes 6148
  1.9 14.8 %copy-start.2 = (bf16[4096,128]{1,0:T(8,128)(2,1)S(1)}, bf16[4096,128]{1,0:T(8,128)(2,1)}, u32[]{:S(2)}) copy-start(bf16[4096,128]{1,0:T(8,128)(2,1)} %param.12) | copy-start | bytes 3145732
  2.0 14.8 %copy-start.4 = (bf16[4096,128]{1,0:T(8,128)(2,1)S(1)}, bf16[4096,128]{1,0:T(8,128)(2,1)}, u32[]{:S(2)}) copy-start(bf16[4096,128]{1,0:T(8,128)(2,1)} %param.11) | copy-start | bytes 3145732
  9.5 33.0 %all-to-all-start.1 = ((bf16[8,128,512]{2,1,0:T(8,128)(2,1)}), bf16[8,128,512]{2,1,0:T(8,128)(2,1)S(1)}, u32[]{:S(2)}, u32[]{:S(2)}) async-start(bf16[8,128,512]{2,1,0:T(8,128)(2,1)} %bitcast.162), calls=%async_computation.1 | async-start | bytes 2097152 | tf_op jit(solution)/shard_map/all_to_all | solution.py:359
  16.8 3.6 %copy-start.11 = (s32[512]{0:T(512)S(1)}, s32[512]{0:T(512)}, u32[]{:S(2)}) copy-start(s32[512]{0:T(512)} %param.16) | copy-start | bytes 6148
  16.8 4.1 %copy-start.10 = (s32[512]{0:T(512)S(1)}, s32[512]{0:T(512)}, u32[]{:S(2)}) copy-start(s32[512]{0:T(512)} %param.15) | copy-start | bytes 6148
  23.6 6.1 %copy-start.13 = (s32[512]{0:T(512)S(1)}, s32[512]{0:T(512)}, u32[]{:S(2)}) copy-start(s32[512]{0:T(512)} %copy-done.12) | copy-start | bytes 6148
  42.5 40.8 %all-to-all-start = ((bf16[8,128,768]{2,1,0:T(8,128)(2,1)}), bf16[8,128,768]{2,1,0:T(8,128)(2,1)S(1)}, u32[]{:S(2)}, u32[]{:S(2)}) async-start(bf16[8,128,768]{2,1,0:T(8,128)(2,1)} %bitcast.9), calls=%async_computation | async-start | bytes 3145728 | tf_op jit(solution)/shard_map/all_to_all | solution.py:359
  46.5 49.5 %copy-start.15 = (s32[512]{0:T(512)}, s32[512]{0:T(512)S(1)}, u32[]{:S(2)}) copy-start(s32[512]{0:T(512)S(1)} %add.139) | copy-start | bytes 6148
  84.4 0.9 copy-start.7
  85.6 2.9 %copy-start.17 = (bf16[512,512]{0,1:T(8,128)(2,1)S(1)}, bf16[512,512]{0,1:T(8,128)(2,1)}, u32[]{:S(2)}) copy-start(bf16[512,512]{0,1:T(8,128)(2,1)} %fusion.38) | copy-start | bytes 1572868
  87.4 3.8 %copy-start = (f32[512,512,4]{1,0,2:T(8,128)}, f32[512,512,4]{1,0,2:T(8,128)S(1)}, u32[]{:S(2)}) copy-start(f32[512,512,4]{1,0,2:T(8,128)S(1)} %get-tuple-element.25) | copy-start | bytes 12582916
  88.5 2.7 copy-start.8
  97.8 7.7 %copy-start.9 = (f32[4,512]{1,0:T(4,128)S(1)}, f32[4,512]{1,0:T(4,128)}, u32[]{:S(2)}) copy-start(f32[4,512]{1,0:T(4,128)} %copy-done.8) | copy-start | bytes 24580
  97.8 29.7 %all-to-all-start.3 = ((bf16[8,128,512]{2,1,0:T(8,128)(2,1)}), bf16[8,128,512]{2,1,0:T(8,128)(2,1)S(1)}, u32[]{:S(2)}, u32[]{:S(2)}) async-start(bf16[8,128,512]{2,1,0:T(8,128)(2,1)} %bitcast.164), calls=%async_computation.3 | async-start | bytes 2097152 | tf_op jit(solution)/shard_map/all_to_all | solution.py:359
  101.5 4.0 %copy-start.1 = (f32[512,512,4]{1,0,2:T(8,128)S(1)}, f32[512,512,4]{1,0,2:T(8,128)}, u32[]{:S(2)}) copy-start(f32[512,512,4]{1,0,2:T(8,128)} %copy-done) | copy-start | bytes 12582916
  101.5 4.0 %copy-start.18 = (bf16[512,512]{0,1:T(8,128)(2,1)S(1)}, bf16[512,512]{0,1:T(8,128)(2,1)}, u32[]{:S(2)}) copy-start(bf16[512,512]{0,1:T(8,128)(2,1)} %fusion.38) | copy-start | bytes 1572868
  105.5 1.5 copy-start.16
  127.5 3.8 %copy-start.5 = (bf16[8,128,512]{2,1,0:T(8,128)(2,1)}, bf16[8,128,512]{2,1,0:T(8,128)(2,1)S(1)}, u32[]{:S(2)}) copy-start(bf16[8,128,512]{2,1,0:T(8,128)(2,1)S(1)} %all-to-all-done.3) | copy-start | bytes 3145732
  127.5 40.9 %all-to-all-start.2 = ((bf16[8,128,768]{2,1,0:T(8,128)(2,1)}), bf16[8,128,768]{2,1,0:T(8,128)(2,1)S(1)}, u32[]{:S(2)}, u32[]{:S(2)}) async-start(bf16[8,128,768]{2,1,0:T(8,128)(2,1)} %bitcast.46), calls=%async_computation.2 | async-start | bytes 3145728 | tf_op jit(solution)/shard_map/all_to_all | solution.py:359
  137.8 6.6 %copy-start.3 = (bf16[4096,128]{1,0:T(8,128)(2,1)S(1)}, bf16[4096,128]{1,0:T(8,128)(2,1)}, u32[]{:S(2)}) copy-start(bf16[4096,128]{1,0:T(8,128)(2,1)} %param.12) | copy-start | bytes 3145732
  144.4 6.1 %copy-start.6 = (bf16[8,128,512]{2,1,0:T(8,128)(2,1)S(1)}, bf16[8,128,512]{2,1,0:T(8,128)(2,1)}, u32[]{:S(2)}) copy-start(bf16[8,128,512]{2,1,0:T(8,128)(2,1)} %copy-done.5) | copy-start | bytes 3145732
  144.4 6.1 %copy-start.14 = (s32[512]{0:T(512)S(1)}, s32[512]{0:T(512)}, u32[]{:S(2)}) copy-start(s32[512]{0:T(512)} %copy-done.12) | copy-start | bytes 6148
